TPU v7x, 512 devices: a whole 4x4x16 slice. The times are simulated.
512 devices in a mesh: dom: 64 (over x, z), rep: 8 (over y, core).
Axes of the slice: x: 4, y: 4, z: 16, core: 2. Of those that a mesh axis runs over, the one named last changes fastest.
Arguments:
- history: bfloat16 [2, 524288, 256], P(None, ('dom', 'rep')), may hold values from -6 to 6
- tile_values: bfloat16 [4096, 8, 128, 128], P(('dom', 'rep')), may hold values from -0.5 to 0.5
- tile_cols: int32 [4096, 8], P(('dom', 'rep')), may hold values from 0 to 11, all different within a row
- send_rows: int32 [512, 64, 8], P(('dom', 'rep')), may hold values from 0 to 1023
- send_count: int32 [512, 64], P(('dom', 'rep')), may hold values from 1 to 8, as said below
- node_ids: int32 [512, 1024], P(('dom', 'rep')), may hold values from 0 to 1023, each once within a row
- weights: bfloat16 [2, 256, 256], replicated, may hold values from -0.375 to 0.375
- upstream: bfloat16 [524288, 256], P(('dom', 'rep'))
Outputs:
- history_out: bfloat16 [1, 524288, 256], P(None, ('dom', 'rep'))
- weight_grads: float32 [2, 256, 256], replicated
Inputs may be any that keep to these rules, and one draw needn't show every extreme that they name: In each list the first send_count entries are live and the rest empty; in every draw each device has a list of 8 live entries. `tile_cols`: each row block names 8 different column blocks; blocks below 8 hold batch rows, the others halo slots.
All inputs are finite; a program needn't handle non-finite values.
Results may differ from a plain program's by a relative error of at most 0.0065.
Values may be sent and summed in bfloat16 or wider, within the bound.
A program may use at most 64 MiB of HBM per device.

v0:
```python
import math
import jax
import jax.numpy as jnp
from jax import lax
from jax.sharding import PartitionSpec as P

RESTART = 0.1


def layer_beta(level):
    return math.log(0.5 / (level + 1) + 1.0)


def silu_slope(preact):
    sigma = jax.nn.sigmoid(preact)
    return sigma * (1.0 + preact * (1.0 - sigma))


def outgoing(layer_table, send_rows, send_count):
    picked = jnp.take(layer_table, send_rows[0], axis=0)
    slot_index = lax.broadcasted_iota(jnp.int32, send_rows.shape[1:], 1)
    live_mask = slot_index < send_count[0][:, None]
    return jnp.where(live_mask[:, :, None], picked, jnp.zeros_like(picked))


def aggregate(tiles, tile_cols, node_table):
    tile_size = tiles.shape[2]
    blocks = node_table.reshape(-1, tile_size, node_table.shape[1])
    picked = jnp.take(blocks, tile_cols, axis=0)
    summed = jnp.einsum("rtij,rtjf->rif", tiles, picked, preferred_element_type=jnp.float32)
    return summed.reshape(-1, node_table.shape[1])


def spread_back(tiles, tile_cols, back_rows, batch_rows):
    tile_size = tiles.shape[2]
    blocks = back_rows.reshape(-1, tile_size, back_rows.shape[1])
    pieces = jnp.einsum("rtij,rif->rtjf", tiles, blocks, preferred_element_type=jnp.float32)
    targets = lax.broadcasted_iota(jnp.int32, (1, 1, batch_rows // tile_size), 2)
    owners = (tile_cols[:, :, None] == targets).astype(jnp.float32)
    placed = jnp.einsum("rtc,rtjf->cjf", owners, pieces, precision=lax.Precision.HIGHEST)
    return placed.reshape(batch_rows, back_rows.shape[1])


def local(history, tile_values, tile_cols, send_rows, send_count, node_ids, weights, upstream):
    levels = history.shape[0]
    batch_rows = history.shape[1]
    feature_width = history.shape[2]
    node_rows = node_ids[0]
    h_start = jnp.take(history[0], node_rows, axis=0)
    halos = [
        lax.all_to_all(
            outgoing(history[level], send_rows, send_count),
            "dom",
            split_axis=0,
            concat_axis=0,
            tiled=True,
        ).reshape(-1, feature_width)
        for level in range(levels)
    ]
    current = h_start
    mixed_all = []
    preact_all = []
    written = []
    for level in range(levels):
        node_table = jnp.concatenate([current, halos[level]], axis=0)
        summed = aggregate(tile_values, tile_cols, node_table)
        mixed_rows = ((1.0 - RESTART) * summed + RESTART * h_start.astype(jnp.float32)).astype(
            jnp.bfloat16
        )
        beta_value = layer_beta(level)
        preact = (1.0 - beta_value) * mixed_rows.astype(jnp.float32) + beta_value * jnp.dot(
            mixed_rows, weights[level], preferred_element_type=jnp.float32
        )
        current = jax.nn.silu(preact).astype(jnp.bfloat16)
        mixed_all.append(mixed_rows)
        preact_all.append(preact)
        if level + 1 < levels:
            written.append(
                jnp.zeros((batch_rows, feature_width), jnp.bfloat16).at[node_rows].set(current)
            )
    grads = [None] * levels
    grad_rows = (upstream.astype(jnp.float32) * silu_slope(preact_all[-1])).astype(jnp.bfloat16)
    for level in reversed(range(levels)):
        beta_value = layer_beta(level)
        local_grad = beta_value * jnp.dot(
            mixed_all[level].T, grad_rows, preferred_element_type=jnp.float32
        )
        grads[level] = local_grad
        if level > 0:
            back_rows = (
                (1.0 - beta_value) * grad_rows.astype(jnp.float32)
                + beta_value
                * jnp.dot(grad_rows, weights[level].T, preferred_element_type=jnp.float32)
            ).astype(jnp.bfloat16)
            delta = (1.0 - RESTART) * spread_back(tile_values, tile_cols, back_rows, batch_rows)
            grad_rows = (delta * silu_slope(preact_all[level - 1])).astype(jnp.bfloat16)
    stacked = jnp.stack(grads)
    stacked = lax.psum(stacked, ("dom", "rep"))
    nodes_all = batch_rows * lax.axis_size("dom") * lax.axis_size("rep")
    return (jnp.stack(written), stacked * (1.0 / math.sqrt(nodes_all)))


def solution(mesh):
    return jax.shard_map(
        local,
        mesh=mesh,
        in_specs=(
            P(None, ("dom", "rep"), None),
            P(("dom", "rep"), None, None, None),
            P(("dom", "rep"), None),
            P(("dom", "rep"), None, None),
            P(("dom", "rep"), None),
            P(("dom", "rep"), None),
            P(),
            P(("dom", "rep"), None),
        ),
        out_specs=(P(None, ("dom", "rep"), None), P()),
        check_vma=False,
    )
```

profile of v0, /device:TPU:4, one launch (start us, length us, event | category | flops | bytes accessed | tf_op | source)
XLA Modules:
  0.0 560.6 jit_solution(8905946658000197402)
XLA Ops:
  7.2 0.7 compare_and_fusion.1
  7.9 0.7 compare_select_fusion.2
  8.5 0.1 copy.13
  8.7 0.7 iota_compare_fusion.1
  9.4 0.1 copy.14
  9.5 0.1 reshape.169
  9.6 0.0 copy-start.6
  9.6 0.0 copy-start.7
  9.6 1.3 slice_bitcast_fusion
  10.9 2.0 gather_fusion.3
  12.9 2.0 gather_fusion.1
  14.8 1.0 fusion.39
  15.8 18.7 %all-to-all-start = ((bf16[64,8,256]{2,1,0:T(8,128)(2,1)}), bf16[64,8,256]{2,1,0:T(8,128)(2,1)S(1)}, u32[]{:S(2)}, u32[]{:S(2)}) async-start(bf16[64,8,256]{2,1,0:T(8,128)(2,1)} %get-tuple-element.7), calls=%async_computation | async-start | bytes 524288 | tf_op jit(solution)/shard_map/all_to_all | solution.py:51
  34.6 0.1 reshape.173
  34.7 3.9 gather_fusion
  38.6 2.9 copy.20
  41.6 0.2 broadcast_select_fusion
  41.8 13.6 %all-to-all-done = bf16[64,8,256]{2,1,0:T(8,128)(2,1)S(1)} async-done(((bf16[64,8,256]{2,1,0:T(8,128)(2,1)}), bf16[64,8,256]{2,1,0:T(8,128)(2,1)S(1)}, u32[]{:S(2)}, u32[]{:S(2)}) %all-to-all-start) | async-done | bytes 262176 | tf_op jit(solution)/shard_map/all_to_all | solution.py:51
  55.3 6.8 %all-to-all-start.1 = ((bf16[64,8,256]{2,1,0:T(8,128)(2,1)}), bf16[64,8,256]{2,1,0:T(8,128)(2,1)}, u32[]{:S(2)}, u32[]{:S(2)}) async-start(bf16[64,8,256]{2,1,0:T(8,128)(2,1)} %get-tuple-element.6), calls=%async_computation.1 | async-start | bytes 524288 | tf_op jit(solution)/shard_map/all_to_all | solution.py:51
  62.2 0.2 all-reduce.2.cloned.1.call-start
  62.4 0.1 pad_maximum_fusion
  62.5 0.0 copy-start.1
  62.5 2.8 gather_fusion.2
  65.2 3.0 fusion.38
  68.3 0.2 fusion.35
  68.5 0.0 copy-start.4
  68.5 0.8 copy-done.4
  69.3 1.6 multiply_convert_fusion.1
  70.9 11.3 %all-to-all-done.1 = bf16[64,8,256]{2,1,0:T(8,128)(2,1)} async-done(((bf16[64,8,256]{2,1,0:T(8,128)(2,1)}), bf16[64,8,256]{2,1,0:T(8,128)(2,1)}, u32[]{:S(2)}, u32[]{:S(2)}) %all-to-all-start.1) | async-done | bytes 262176 | tf_op jit(solution)/shard_map/all_to_all | solution.py:51
  82.2 1.2 pad_maximum_fusion.1
  83.4 2.8 gather_fusion.4
  86.1 3.0 fusion.37
  89.2 0.2 fusion.34
  89.5 0.7 multiply_convert_fusion
  90.1 0.3 fusion.32
  90.5 0.3 fusion.31
  90.8 0.2 copy-done.2
  91.1 1.2 fusion.54
  92.3 5.6 fusion.28
  97.9 0.3 copy.17
  98.2 0.3 fusion.36
  98.6 0.3 copy-done.5
  98.9 0.3 fusion.33
  99.2 0.8 pad_maximum_fusion.2
  100.1 0.0 all-reduce.2.cloned.1.call-update
  100.1 6.1 %scatter_custom_fusion = bf16[1024,256]{1,0:T(8,128)(2,1)} fusion(s32[1024]{0:T(1024)S(1)} %bitcast.119, bf16[1024,256]{1,0:T(8,128)(2,1)} %get-tuple-element.10, bf16[]{:T(256)} %constant.29.clone.1), kind=kCustom, calls=%fused_computation.60 | custom fusion | bytes 524800 | tf_op jit(solution)/shard_map/scatter | solution.py:79
  106.2 445.7 %all-reduce.2.cloned.1.call-done = f32[2,256,256]{2,1,0:T(8,128)} async-done(((f32[2,256,256]{2,1,0:T(8,128)}), f32[2,256,256]{2,1,0:T(8,128)}) %all-reduce.2.cloned.1.call-update) | async-done | bytes 524304 | tf_op jit(solution)/shard_map/psum | solution.py:98
  551.9 1.9 broadcast_multiply_fusion
  (23 shorter events, 0.1 us)
Async XLA Ops:
  9.6 25.0 %copy-start.6 = (s32[8,8]{1,0:T(8,128)S(1)}, s32[8,8]{1,0:T(8,128)}, u32[]{:S(2)}) copy-start(s32[8,8]{1,0:T(8,128)} %param.14) | copy-start | bytes 772
  9.6 25.0 %copy-start.7 = (s32[1,1024]{1,0:T(1,128)S(1)}, s32[1,1024]{1,0:T(1,128)}, u32[]{:S(2)}) copy-start(s32[1,1024]{1,0:T(1,128)} %param.17) | copy-start | bytes 12292
  12.8 25.8 %copy-start = (bf16[8,8,128,128]{3,2,1,0:T(8,128)(2,1)S(1)}, bf16[8,8,128,128]{3,2,1,0:T(8,128)(2,1)}, u32[]{:S(2)}) copy-start(bf16[8,8,128,128]{3,2,1,0:T(8,128)(2,1)} %param.13) | copy-start | bytes 6291460
  15.8 39.5 %all-to-all-start = ((bf16[64,8,256]{2,1,0:T(8,128)(2,1)}), bf16[64,8,256]{2,1,0:T(8,128)(2,1)S(1)}, u32[]{:S(2)}, u32[]{:S(2)}) async-start(bf16[64,8,256]{2,1,0:T(8,128)(2,1)} %get-tuple-element.7), calls=%async_computation | async-start | bytes 524288 | tf_op jit(solution)/shard_map/all_to_all | solution.py:51
  55.3 26.8 %all-to-all-start.1 = ((bf16[64,8,256]{2,1,0:T(8,128)(2,1)}), bf16[64,8,256]{2,1,0:T(8,128)(2,1)}, u32[]{:S(2)}, u32[]{:S(2)}) async-start(bf16[64,8,256]{2,1,0:T(8,128)(2,1)} %get-tuple-element.6), calls=%async_computation.1 | async-start | bytes 524288 | tf_op jit(solution)/shard_map/all_to_all | solution.py:51
  62.2 489.7 %all-reduce.2.cloned.1.call-start = ((), (), s32[]{:S(2)}) async-start(), calls=%async_computation.2 | async-start | bytes 1048576 | tf_op jit(solution)/shard_map/psum | solution.py:98
  62.5 2.8 copy-start.1
  65.2 4.1 copy-start.9
  68.5 0.8 copy-start.4
  86.1 3.3 copy-start.8
  86.1 3.3 copy-start.10
  89.5 1.6 copy-start.2
  92.3 5.9 %copy-start.3 = (f32[1024,256]{1,0:T(8,128)S(1)}, f32[1024,256]{1,0:T(8,128)}, u32[]{:S(2)}) copy-start(f32[1024,256]{1,0:T(8,128)} %get-tuple-element.11) | copy-start | bytes 3145732
  97.9 1.1 copy-start.5
Sparse Core Ops, SparseCore 0:
  100.2 451.6 all-reduce.1
where the time goes:
time: 561 us
  waiting for transfers between devices  471 us (84%)
  local copies, waits for them, and re-layouts  25.8 us (5%)
  starting transfers between devices  25.7 us (5%)
  matrix products  16.1 us (3%)
  between operations  14.3 us (3%)
  other arithmetic  8.14 us (1%)
    psum x1, waiting for transfers between devices, local(): stacked = lax.psum(stacked, ('dom', 'rep'))  446 us
    all_to_all x2, starting transfers between devices, local(): lax.all_to_all(outgoing(history[level], send_rows, send_count), 'dom', sp...  25.5 us
    all_to_all x2, waiting for transfers between devices, local(): lax.all_to_all(outgoing(history[level], send_rows, send_count), 'dom', sp...  24.8 us
  transfers between devices with their start and end apart: 3, of which 3 were waited for; matrix products, arithmetic and copies ran while one was open for 4% of the time, Pallas kernels for 0%

commit v1 on v0

--- a/solution.py
+++ b/solution.py
@@ -95,7 +95,7 @@
             delta = (1.0 - RESTART) * spread_back(tile_values, tile_cols, back_rows, batch_rows)
             grad_rows = (delta * silu_slope(preact_all[level - 1])).astype(jnp.bfloat16)
     stacked = jnp.stack(grads)
-    stacked = lax.psum(stacked, ("dom", "rep"))
+    stacked = lax.psum(lax.psum(stacked, "dom"), "rep")
     nodes_all = batch_rows * lax.axis_size("dom") * lax.axis_size("rep")
     return (jnp.stack(written), stacked * (1.0 / math.sqrt(nodes_all)))
 

time: 561 us -> 441 us (0.79)
  the two profiles are of different devices: /device:TPU:4 before, /device:TPU:2 now
where the time goes in v1:
time: 441 us; the launch traced here: 440 us
  waiting for transfers between devices  350 us (79%)
  starting transfers between devices  25.9 us (6%)
  local copies, waits for them, and re-layouts  25.8 us (6%)
  matrix products  16.1 us (4%)
  between operations  14.3 us (3%)
  other arithmetic  8.13 us (2%)
    psum x2, waiting for transfers between devices, local(): stacked = lax.psum(lax.psum(stacked, 'dom'), 'rep')  325 us
    all_to_all x2, starting transfers between devices, local(): lax.all_to_all(outgoing(history[level], send_rows, send_count), 'dom', sp...  25.4 us
    all_to_all x2, waiting for transfers between devices, local(): lax.all_to_all(outgoing(history[level], send_rows, send_count), 'dom', sp...  24.9 us
  transfers between devices with their start and end apart: 4, of which 4 were waited for; matrix products, arithmetic and copies ran while one was open for 5% of the time, Pallas kernels for 0%

profile of v1, /device:TPU:2, one launch (start us, length us, event | category | flops | bytes accessed | tf_op | source)
XLA Modules:
  0.0 440.4 jit_solution(16094793235458402484)
XLA Ops:
  7.2 0.7 compare_and_fusion.1
  7.9 0.7 compare_select_fusion.2
  8.5 0.1 copy.13
  8.7 0.7 iota_compare_fusion.1
  9.4 0.1 copy.14
  9.5 0.1 reshape.169
  9.6 0.0 copy-start.6
  9.6 1.3 slice_bitcast_fusion
  10.9 2.0 gather_fusion.3
  12.9 2.0 gather_fusion.1
  14.8 1.0 fusion.39
  15.8 18.6 %all-to-all-start = ((bf16[64,8,256]{2,1,0:T(8,128)(2,1)}), bf16[64,8,256]{2,1,0:T(8,128)(2,1)S(1)}, u32[]{:S(2)}, u32[]{:S(2)}) async-start(bf16[64,8,256]{2,1,0:T(8,128)(2,1)} %get-tuple-element.7), calls=%async_computation | async-start | bytes 524288 | tf_op jit(solution)/shard_map/all_to_all | solution.py:51
  34.5 0.1 reshape.173
  34.6 3.9 gather_fusion
  38.6 2.9 copy.20
  41.5 0.2 broadcast_select_fusion
  41.7 13.6 %all-to-all-done = bf16[64,8,256]{2,1,0:T(8,128)(2,1)S(1)} async-done(((bf16[64,8,256]{2,1,0:T(8,128)(2,1)}), bf16[64,8,256]{2,1,0:T(8,128)(2,1)S(1)}, u32[]{:S(2)}, u32[]{:S(2)}) %all-to-all-start) | async-done | bytes 262176 | tf_op jit(solution)/shard_map/all_to_all | solution.py:51
  55.3 6.8 %all-to-all-start.1 = ((bf16[64,8,256]{2,1,0:T(8,128)(2,1)}), bf16[64,8,256]{2,1,0:T(8,128)(2,1)}, u32[]{:S(2)}, u32[]{:S(2)}) async-start(bf16[64,8,256]{2,1,0:T(8,128)(2,1)} %get-tuple-element.6), calls=%async_computation.1 | async-start | bytes 524288 | tf_op jit(solution)/shard_map/all_to_all | solution.py:51
  62.1 0.2 all-reduce.3.cloned.1.call-start
  62.3 0.1 pad_maximum_fusion
  62.4 2.8 gather_fusion.2
  65.2 3.0 fusion.38
  68.2 0.2 fusion.35
  68.5 0.8 copy-done.4
  69.2 1.6 multiply_convert_fusion.1
  70.9 11.3 %all-to-all-done.1 = bf16[64,8,256]{2,1,0:T(8,128)(2,1)} async-done(((bf16[64,8,256]{2,1,0:T(8,128)(2,1)}), bf16[64,8,256]{2,1,0:T(8,128)(2,1)}, u32[]{:S(2)}, u32[]{:S(2)}) %all-to-all-start.1) | async-done | bytes 262176 | tf_op jit(solution)/shard_map/all_to_all | solution.py:51
  82.1 1.2 pad_maximum_fusion.1
  83.3 2.8 gather_fusion.4
  86.1 3.0 fusion.37
  89.1 0.2 fusion.34
  89.4 0.6 multiply_convert_fusion
  90.1 0.3 fusion.32
  90.4 0.3 fusion.31
  90.8 0.2 copy-done.2
  91.0 1.2 fusion.54
  92.2 5.6 %fusion.28 = f32[8,128,256]{2,0,1:T(8,128)S(1)} fusion(f32[8,256,8,128]{1,2,0,3:T(8,128)S(1)} %fusion.54, s32[8,8]{1,0:T(8,128)S(1)} %copy-done.6), kind=kOutput, calls=%fused_computation.27 | convolution fusion | flops 201589248 | bytes 9437440 | tf_op jit(solution)/shard_map/rtc,rtjf->cjf/dot_general | solution.py:40
  97.8 0.3 copy.17
  98.2 0.3 fusion.36
  98.5 0.3 copy-done.5
  98.8 0.3 fusion.33
  99.2 0.8 pad_maximum_fusion.2
  100.0 0.0 all-reduce.3.cloned.1.call-update
  100.0 0.3 all-reduce.5.cloned.1.call-start
  100.3 257.0 %all-reduce.3.cloned.1.call-done = f32[2,256,256]{2,1,0:T(8,128)} async-done(((f32[2,256,256]{2,1,0:T(8,128)}), f32[2,256,256]{2,1,0:T(8,128)}) %all-reduce.3.cloned.1.call-update) | async-done | bytes 524304 | tf_op jit(solution)/shard_map/psum | solution.py:98
  357.4 0.0 all-reduce.5.cloned.1.call-update
  357.4 6.1 %scatter_custom_fusion = bf16[1024,256]{1,0:T(8,128)(2,1)} fusion(s32[1024]{0:T(1024)S(1)} %bitcast.119, bf16[1024,256]{1,0:T(8,128)(2,1)} %get-tuple-element.10, bf16[]{:T(256)} %constant.29.clone.1), kind=kCustom, calls=%fused_computation.60 | custom fusion | bytes 524800 | tf_op jit(solution)/shard_map/scatter | solution.py:79
  363.5 68.2 %all-reduce.5.cloned.1.call-done = f32[2,256,256]{2,1,0:T(8,128)} async-done(((f32[2,256,256]{2,1,0:T(8,128)}), f32[2,256,256]{2,1,0:T(8,128)}) %all-reduce.5.cloned.1.call-update) | async-done | bytes 524304 | tf_op jit(solution)/shard_map/psum | solution.py:98
  431.7 1.9 broadcast_multiply_fusion
  (26 shorter events, 0.1 us)
Async XLA Ops:
  9.6 24.9 %copy-start.6 = (s32[8,8]{1,0:T(8,128)S(1)}, s32[8,8]{1,0:T(8,128)}, u32[]{:S(2)}) copy-start(s32[8,8]{1,0:T(8,128)} %param.14) | copy-start | bytes 772
  9.6 25.0 %copy-start.7 = (s32[1,1024]{1,0:T(1,128)S(1)}, s32[1,1024]{1,0:T(1,128)}, u32[]{:S(2)}) copy-start(s32[1,1024]{1,0:T(1,128)} %param.17) | copy-start | bytes 12292
  12.8 25.7 %copy-start = (bf16[8,8,128,128]{3,2,1,0:T(8,128)(2,1)S(1)}, bf16[8,8,128,128]{3,2,1,0:T(8,128)(2,1)}, u32[]{:S(2)}) copy-start(bf16[8,8,128,128]{3,2,1,0:T(8,128)(2,1)} %param.13) | copy-start | bytes 6291460
  15.8 39.5 %all-to-all-start = ((bf16[64,8,256]{2,1,0:T(8,128)(2,1)}), bf16[64,8,256]{2,1,0:T(8,128)(2,1)S(1)}, u32[]{:S(2)}, u32[]{:S(2)}) async-start(bf16[64,8,256]{2,1,0:T(8,128)(2,1)} %get-tuple-element.7), calls=%async_computation | async-start | bytes 524288 | tf_op jit(solution)/shard_map/all_to_all | solution.py:51
  55.3 26.8 %all-to-all-start.1 = ((bf16[64,8,256]{2,1,0:T(8,128)(2,1)}), bf16[64,8,256]{2,1,0:T(8,128)(2,1)}, u32[]{:S(2)}, u32[]{:S(2)}) async-start(bf16[64,8,256]{2,1,0:T(8,128)(2,1)} %get-tuple-element.6), calls=%async_computation.1 | async-start | bytes 524288 | tf_op jit(solution)/shard_map/all_to_all | solution.py:51
  62.1 295.3 %all-reduce.3.cloned.1.call-start = ((), (), s32[]{:S(2)}) async-start(), calls=%async_computation.2 | async-start | bytes 1048576 | tf_op jit(solution)/shard_map/psum | solution.py:98
  62.4 2.8 copy-start.1
  65.2 4.1 copy-start.9
  68.4 0.8 copy-start.4
  86.1 3.3 copy-start.8
  86.1 3.3 copy-start.10
  89.4 1.6 copy-start.2
  92.2 5.9 %copy-start.3 = (f32[1024,256]{1,0:T(8,128)S(1)}, f32[1024,256]{1,0:T(8,128)}, u32[]{:S(2)}) copy-start(f32[1024,256]{1,0:T(8,128)} %get-tuple-element.11) | copy-start | bytes 3145732
  97.8 1.1 copy-start.5
  100.0 331.6 %all-reduce.5.cloned.1.call-start = ((), (), s32[]{:S(2)}) async-start(), calls=%async_computation.3 | async-start | bytes 1048576 | tf_op jit(solution)/shard_map/psum | solution.py:98
Sparse Core Ops, SparseCore 0:
  100.2 257.1 all-reduce.2
  359.8 71.8 all-reduce.4
